TPU v7x, 32 devices: a whole 2x2x4 slice. The times are simulated.
32 devices in a mesh: groups: 2 (over x), replica: 8 (over z, y), tensor: 2 (over core).
Axes of the slice: x: 2, y: 2, z: 4, core: 2. Of those that a mesh axis runs over, the one named last changes fastest.
Arguments:
- cache_keys: bfloat16 [192, 128, 2560], P(('groups', 'replica'), None, 'tensor'), parts along dimension 0, may hold values from -6 to 6
- cache_values: bfloat16 [192, 128, 2560], P(('groups', 'replica'), None, 'tensor'), parts along dimension 0, may hold values from -6 to 6
- lengths: int32 [192], P(('groups', 'replica')), parts along dimension 0, may hold values from 1 to 128, 6144 in all
- new_slot: int32 [192], P(('groups', 'replica')), parts along dimension 0, may hold values from 0 to 95, as said below
- query_raw: bfloat16 [192, 32, 2560], P(('groups', 'replica'), None, 'tensor'), parts along dimension 0, may hold values from -1000 to 1000
- block_keys_raw: bfloat16 [192, 32, 2560], P(('groups', 'replica'), None, 'tensor'), parts along dimension 0, may hold values from -1000 to 1000
- block_values: bfloat16 [192, 32, 2560], P(('groups', 'replica'), None, 'tensor'), parts along dimension 0, may hold values from -6 to 6
- query_gain: bfloat16 [2560], P('tensor'), may hold values from 0.5 to 1.5
- key_gain: bfloat16 [2560], P('tensor'), may hold values from 0.5 to 1.5
Outputs:
- attended: bfloat16 [192, 32, 2560], P(('groups', 'replica'), None, 'tensor'), parts along dimension 0
There are 2 independent parts, one for each index of `groups`. A program takes and returns all parts, laid end to end along the dimension named above; an argument that names none is the same for every part. Nothing has to cross between parts.
Inputs may be any that keep to these rules, and one draw needn't show every extreme that they name: new_slot is a permutation; slot // 12 is a replica. Of one replica's streams at most 2 go to any one replica (its own included), and some pair of replicas reaches 2. Streams in the same slot position of different replicas go to different replicas.
All inputs are finite; a program needn't handle non-finite values. No bound on the sum of `lengths` on one device may be relied on, other than what follows from the above.
Results may differ from a plain program's by a relative error of at most 0.0083.
Values may be sent and summed in bfloat16 or wider, within the bound.
A program may use at most 128 MiB of HBM per device.

v0:
```python
import jax
import jax.numpy as jnp
from jax import lax
from jax.sharding import PartitionSpec as P

HEAD_DIM = 128


def split_heads(source_rows):
    return source_rows.reshape(
        source_rows.shape[0], source_rows.shape[1], source_rows.shape[2] // HEAD_DIM, HEAD_DIM
    )


def pick_rows(selection, source_rows):
    flattened = source_rows.reshape(source_rows.shape[0], -1)
    picked = jnp.dot(selection, flattened, preferred_element_type=jnp.float32).astype(
        source_rows.dtype
    )
    return picked.reshape((selection.shape[0],) + source_rows.shape[1:])


def own_scores(queries, block_keys):
    return jnp.einsum(
        "sqhd,skhd->shqk",
        split_heads(queries),
        split_heads(block_keys),
        preferred_element_type=jnp.float32,
    ) * HEAD_DIM ** (-0.5)


def finish(queries, own_part, block_vals, past_keys, past_vals, live):
    past_part = jnp.einsum(
        "sqhd,skhd->shqk",
        split_heads(queries),
        split_heads(past_keys),
        preferred_element_type=jnp.float32,
    ) * HEAD_DIM ** (-0.5)
    valid = jnp.arange(past_keys.shape[1], dtype=jnp.int32)[None, :] < live[:, None]
    past_part = jnp.where(valid[:, None, None, :], past_part, -1e30)
    row_max = jnp.maximum(
        jnp.max(past_part, axis=-1, keepdims=True), jnp.max(own_part, axis=-1, keepdims=True)
    )
    past_exp = jnp.exp(past_part - row_max)
    own_exp = jnp.exp(own_part - row_max)
    denominator = jnp.sum(past_exp, axis=-1, keepdims=True) + jnp.sum(
        own_exp, axis=-1, keepdims=True
    )
    past_weights = (past_exp / denominator).astype(jnp.bfloat16)
    own_weights = (own_exp / denominator).astype(jnp.bfloat16)
    result = jnp.einsum(
        "shqk,skhd->sqhd", past_weights, split_heads(past_vals), preferred_element_type=jnp.float32
    )
    result = result + jnp.einsum(
        "shqk,skhd->sqhd", own_weights, split_heads(block_vals), preferred_element_type=jnp.float32
    )
    return result.reshape(queries.shape).astype(jnp.bfloat16)


def local(
    cache_keys,
    cache_values,
    lengths,
    new_slot,
    query_raw,
    block_keys_raw,
    block_values,
    query_gain,
    key_gain,
):
    slot_count = cache_keys.shape[0]
    local_width = cache_keys.shape[2]
    full_width = local_width * lax.axis_size("tensor")
    peer_count = lax.axis_size("replica")
    own_index = lax.axis_index("replica")
    capacity = -(-slot_count // peer_count)
    query_float = query_raw.astype(jnp.float32)
    key_float = block_keys_raw.astype(jnp.float32)
    query_squares, key_squares = lax.psum(
        (jnp.sum(query_float * query_float, axis=-1), jnp.sum(key_float * key_float, axis=-1)),
        "tensor",
    )
    query_normed = (
        query_float
        * lax.rsqrt(query_squares / full_width + 1e-06)[..., None]
        * query_gain.astype(jnp.float32)
    ).astype(jnp.bfloat16)
    key_normed = (
        key_float
        * lax.rsqrt(key_squares / full_width + 1e-06)[..., None]
        * key_gain.astype(jnp.float32)
    ).astype(jnp.bfloat16)
    position = jnp.arange(slot_count, dtype=jnp.int32)
    bucket_ids = jnp.arange(peer_count * capacity, dtype=jnp.int32)
    dest_local = new_slot // slot_count
    earlier = (position[None, :] < position[:, None]) & (dest_local[None, :] == dest_local[:, None])
    rank_local = jnp.sum(earlier.astype(jnp.int32), axis=1)
    send_select = ((dest_local * capacity + rank_local)[None, :] == bucket_ids[:, None]).astype(
        jnp.bfloat16
    )
    all_slots, all_lengths = (
        lax.all_gather(new_slot, "replica", axis=0, tiled=True),
        lax.all_gather(lengths, "replica", axis=0, tiled=True),
    )
    stream_total = all_slots.shape[0]
    dest_board = (all_slots // slot_count).reshape(peer_count, slot_count)
    matches = (dest_board[:, None, :] == dest_board[:, :, None]) & (
        position[None, None, :] < position[None, :, None]
    )
    rank_all = jnp.sum(matches.astype(jnp.int32), axis=2).reshape(stream_total)
    column = jnp.arange(stream_total, dtype=jnp.int32) // slot_count * capacity + rank_all
    arrive = (all_slots[None, :] == own_index * slot_count + position[:, None]).astype(jnp.float32)
    receive_select = jnp.dot(
        arrive,
        (column[:, None] == bucket_ids[None, :]).astype(jnp.float32),
        preferred_element_type=jnp.float32,
    ).astype(jnp.bfloat16)
    live_new = jnp.dot(
        arrive, all_lengths.astype(jnp.float32), preferred_element_type=jnp.float32
    ).astype(jnp.int32)
    own_part = own_scores(query_normed, key_normed)
    outgoing_keys = pick_rows(send_select, cache_keys)
    outgoing_values = pick_rows(send_select, cache_values)
    arrived_keys, arrived_values = (
        lax.all_to_all(outgoing_keys, "replica", split_axis=0, concat_axis=0, tiled=True),
        lax.all_to_all(outgoing_values, "replica", split_axis=0, concat_axis=0, tiled=True),
    )
    moved_keys = pick_rows(receive_select, arrived_keys)
    moved_values = pick_rows(receive_select, arrived_values)
    return finish(query_normed, own_part, block_values, moved_keys, moved_values, live_new)


def solution(mesh):
    in_specs = (
        P(("groups", "replica"), None, "tensor"),
        P(("groups", "replica"), None, "tensor"),
        P(("groups", "replica")),
        P(("groups", "replica")),
        P(("groups", "replica"), None, "tensor"),
        P(("groups", "replica"), None, "tensor"),
        P(("groups", "replica"), None, "tensor"),
        P("tensor"),
        P("tensor"),
    )
    out_specs = P(("groups", "replica"), None, "tensor")
    return jax.shard_map(local, mesh=mesh, in_specs=in_specs, out_specs=out_specs, check_vma=False)
```

profile of v0, /device:TPU:0, one launch (start us, length us, event | category | flops | bytes accessed | tf_op | source)
XLA Modules:
  0.0 309.3 jit_solution(8728518269649953782)
XLA Ops:
  0.0 0.8 and_select_fusion
  0.9 0.7 multiply_add_fusion
  1.6 2.5 pad
  4.2 2.9 copy.40
  7.1 1.5 convolution_convert_fusion.1
  8.6 3.4 %copy.41 = bf16[2,8,128,1280]{3,2,1,0:T(8,128)(2,1)} copy(bf16[2,8,128,1280]{3,1,2,0:T(8,128)(2,1)S(1)} %bitcast.78) | data formatting | bytes 10485760
  12.0 7.9 %all-to-all-start.1 = ((bf16[16,128,1280]{2,1,0:T(8,128)(2,1)}), bf16[16,128,1280]{2,1,0:T(8,128)(2,1)}, u32[]{:S(2)}, u32[]{:S(2)}) async-start(bf16[16,128,1280]{2,1,0:T(8,128)(2,1)} %bitcast.81), calls=%async_computation.1 | async-start | bytes 10485760 | tf_op jit(solution)/shard_map/all_to_all | solution.py:125
  19.8 2.5 pad.1
  22.4 2.9 copy.43
  25.3 1.5 convolution_convert_fusion.3
  26.8 3.5 %copy.44 = bf16[2,8,128,1280]{3,2,1,0:T(8,128)(2,1)} copy(bf16[2,8,128,1280]{3,1,2,0:T(8,128)(2,1)S(1)} %bitcast.75) | data formatting | bytes 10485760
  30.3 105.2 %all-to-all-done.1 = bf16[16,128,1280]{2,1,0:T(8,128)(2,1)} async-done(((bf16[16,128,1280]{2,1,0:T(8,128)(2,1)}), bf16[16,128,1280]{2,1,0:T(8,128)(2,1)}, u32[]{:S(2)}, u32[]{:S(2)}) %all-to-all-start.1) | async-done | bytes 5242912 | tf_op jit(solution)/shard_map/all_to_all | solution.py:125
  135.6 4.8 %all-to-all-start = ((bf16[16,128,1280]{2,1,0:T(8,128)(2,1)}), bf16[16,128,1280]{2,1,0:T(8,128)(2,1)}, u32[]{:S(2)}, u32[]{:S(2)}) async-start(bf16[16,128,1280]{2,1,0:T(8,128)(2,1)} %bitcast.80), calls=%async_computation | async-start | bytes 10485760 | tf_op jit(solution)/shard_map/all_to_all | solution.py:126
  140.4 0.6 dynamic-slice
  142.1 113.4 %all-reduce.2 = (s32[96]{0:T(128)S(1)}, s32[96]{0:T(128)S(1)}) all-reduce(s32[96]{0:T(128)S(1)} %dynamic-update-slice, s32[96]{0:T(128)S(1)} %dynamic-update-slice.1), channel_id=1, replica_groups=mesh['groups'=2,'replica'=8,'tensor'=2] {'replica'}, use_global_device_ids=true, to_apply=%add | all-reduce | flops 192 | bytes 1536
  255.6 0.4 convert_reduce_fusion
  256.2 0.5 fusion.4
  256.6 3.4 %all-reduce.3 = (f32[12,32]{1,0:T(8,128)S(1)}, f32[12,32]{1,0:T(8,128)S(1)}) all-reduce(f32[12,32]{1,0:T(8,128)S(1)} %get-tuple-element.14, f32[12,32]{1,0:T(8,128)S(1)} %get-tuple-element.13), channel_id=1, replica_groups=mesh['groups'=2,'replica'=8,'tensor'=2] {'tensor'}, use_global_device_ids=true, to_apply=%region_6.7 | all-reduce | flops 768 | bytes 6144 | tf_op jit(solution)/shard_map/psum | solution.py:79
  260.6 2.2 multiply_reduce_fusion
  262.8 5.4 %copy.42 = bf16[2,8,128,1280]{3,1,2,0:T(8,128)(2,1)S(1)} copy(bf16[2,8,128,1280]{3,2,1,0:T(8,128)(2,1)} %bitcast.18) | data formatting | bytes 10485760
  268.2 3.8 %convolution_convert_fusion = bf16[12,163840]{1,0:T(8,128)(2,1)} fusion(bf16[12,16]{1,0:T(8,128)(2,1)S(1)} %convolution_convert_fusion.4, bf16[16,163840]{1,0:T(8,128)(2,1)S(1)} %bitcast.79), kind=kOutput, calls=%fused_computation | convolution fusion | flops 64880640 | bytes 9175424 | tf_op jit(solution)/shard_map/dot_general | solution.py:17
  272.0 7.0 %reshape_reshape.7 = bf16[12,128,10,128]{3,2,1,0:T(8,128)(2,1)} reshape(bf16[12,163840]{1,0:T(8,128)(2,1)} %convolution_convert_fusion) | data formatting | bytes 7864320 | tf_op jit(solution)/shard_map/reshape;reshape | solution.py:10
  279.0 5.5 %fusion.11 = (f32[12,10,32]{2,1,0:T(8,128)S(1)}, f32[12,10,32,128]{3,2,1,0:T(8,128)S(1)}) fusion(pred[12,128]{1,0:T(8,128)(4,1)S(1)} %iota_compare_fusion.2, bf16[12,128,10,128]{3,2,1,0:T(8,128)(2,1)} %reshape_reshape.7, bf16[12,32,1280]{2,1,0:T(8,128)(2,1)} %param.13, f32[1280]{0:T(1024)S(1)} %convert_element_type.68, f32[12,32]{1,0:T(8,128)S(1)} %add_rsqrt_fusion.1), kind=kOutput, calls=%fused_computation.26 | convolution fusion | flops 129265920 | bytes 6904832 | tf_op jit(solution)/shard_map/sqhd,skhd->shqk/dot_general | solution.py:33
  284.5 0.6 fusion.12
  285.1 1.2 fusion.15
  286.4 5.4 %copy.45 = bf16[2,8,128,1280]{3,1,2,0:T(8,128)(2,1)S(1)} copy(bf16[2,8,128,1280]{3,2,1,0:T(8,128)(2,1)} %bitcast.25) | data formatting | bytes 10485760
  291.8 3.9 %convolution_convert_fusion.2 = bf16[12,163840]{1,0:T(8,128)(2,1)} fusion(bf16[12,16]{1,0:T(8,128)(2,1)S(1)} %convolution_convert_fusion.4, bf16[16,163840]{1,0:T(8,128)(2,1)S(1)} %bitcast.76), kind=kOutput, calls=%fused_computation.2 | convolution fusion | flops 64880640 | bytes 9175424 | tf_op jit(solution)/shard_map/dot_general | solution.py:17
  295.7 7.0 %reshape_reshape.6 = bf16[12,128,10,128]{3,2,1,0:T(8,128)(2,1)} reshape(bf16[12,163840]{1,0:T(8,128)(2,1)} %convolution_convert_fusion.2) | data formatting | bytes 7864320 | tf_op jit(solution)/shard_map/reshape;reshape | solution.py:10
  302.7 2.3 fusion.22
  305.0 1.0 copy-done.1
  306.1 1.9 fusion.16
  308.0 1.1 copy.79
  (42 shorter events, 1.6 us)
Async XLA Ops:
  0.0 302.7 %copy-start = (bf16[12,32,1280]{2,1,0:T(8,128)(2,1)S(1)}, bf16[12,32,1280]{2,1,0:T(8,128)(2,1)}, u32[]{:S(2)}) copy-start(bf16[12,32,1280]{2,1,0:T(8,128)(2,1)} %param.15) | copy-start | bytes 2949124
  12.0 123.5 %all-to-all-start.1 = ((bf16[16,128,1280]{2,1,0:T(8,128)(2,1)}), bf16[16,128,1280]{2,1,0:T(8,128)(2,1)}, u32[]{:S(2)}, u32[]{:S(2)}) async-start(bf16[16,128,1280]{2,1,0:T(8,128)(2,1)} %bitcast.81), calls=%async_computation.1 | async-start | bytes 10485760 | tf_op jit(solution)/shard_map/all_to_all | solution.py:125
  135.5 4.8 %copy-start.9 = (u32[32]{0:T(128)S(1)}, u32[32]{0:T(128)}, u32[]{:S(2)}) copy-start(u32[32]{0:T(128)} %constant.53) | copy-start | bytes 388
  135.5 6.1 %copy-start.7 = (s32[12]{0:T(128)S(1)}, s32[12]{0:T(128)}, u32[]{:S(2)}) copy-start(s32[12]{0:T(128)} %param.12) | copy-start | bytes 148
  135.5 6.3 %copy-start.8 = (s32[12]{0:T(128)S(1)}, s32[12]{0:T(128)}, u32[]{:S(2)}) copy-start(s32[12]{0:T(128)} %param.11) | copy-start | bytes 148
  135.5 120.0 %copy-start.5 = (bf16[1280]{0:T(1024)(128)(2,1)S(1)}, bf16[1280]{0:T(1024)(128)(2,1)}, u32[]{:S(2)}) copy-start(bf16[1280]{0:T(1024)(128)(2,1)} %param.16) | copy-start | bytes 7684
  135.5 120.6 %copy-start.6 = (bf16[1280]{0:T(1024)(128)(2,1)S(1)}, bf16[1280]{0:T(1024)(128)(2,1)}, u32[]{:S(2)}) copy-start(bf16[1280]{0:T(1024)(128)(2,1)} %param.17) | copy-start | bytes 7684
  135.5 120.6 %copy-start.3 = (bf16[12,32,1280]{2,1,0:T(8,128)(2,1)S(1)}, bf16[12,32,1280]{2,1,0:T(8,128)(2,1)}, u32[]{:S(2)}) copy-start(bf16[12,32,1280]{2,1,0:T(8,128)(2,1)} %param.14) | copy-start | bytes 2949124
  135.5 120.6 %copy-start.4 = (bf16[12,32,1280]{2,1,0:T(8,128)(2,1)S(1)}, bf16[12,32,1280]{2,1,0:T(8,128)(2,1)}, u32[]{:S(2)}) copy-start(bf16[12,32,1280]{2,1,0:T(8,128)(2,1)} %param.13) | copy-start | bytes 2949124
  135.6 150.8 %all-to-all-start = ((bf16[16,128,1280]{2,1,0:T(8,128)(2,1)}), bf16[16,128,1280]{2,1,0:T(8,128)(2,1)}, u32[]{:S(2)}, u32[]{:S(2)}) async-start(bf16[16,128,1280]{2,1,0:T(8,128)(2,1)} %bitcast.80), calls=%async_computation | async-start | bytes 10485760 | tf_op jit(solution)/shard_map/all_to_all | solution.py:126
  279.0 5.5 %copy-start.2 = (f32[12,10,32,32]{2,3,1,0:T(8,128)S(1)}, f32[12,10,32,32]{2,3,1,0:T(8,128)}, u32[]{:S(2)}) copy-start(f32[12,10,32,32]{2,3,1,0:T(8,128)} %get-tuple-element.12) | copy-start | bytes 1474564
  302.7 3.4 %copy-start.1 = (bf16[12,128,10,128]{3,2,1,0:T(8,128)(2,1)S(1)}, bf16[12,128,10,128]{3,2,1,0:T(8,128)(2,1)}, u32[]{:S(2)}) copy-start(bf16[12,128,10,128]{3,2,1,0:T(8,128)(2,1)} %reshape_reshape.6) | copy-start | bytes 11796484
where the time goes:
time: 315 us; the launch traced here: 309 us
  blocking collectives  117 us (37%)
  waiting for transfers between devices  105 us (33%)
  local copies, waits for them, and re-layouts  46.1 us (15%)
  matrix products  23 us (7%)
  starting transfers between devices  12.6 us (4%)
  other arithmetic  4.44 us (1%)
    unnamed x1, blocking collectives  113 us
    all_to_all x1, waiting for transfers between devices, local(): lax.all_to_all(outgoing_keys, 'replica', split_axis=0, concat_axis=0, til...  105 us
    unnamed x33, local copies, waits for them, and re-layouts  30.7 us
    another operation x2, local copies, waits for them, and re-layouts, split_heads(): source_rows.reshape(source_rows.shape[0], source_rows.shape[1], source_ro...  14 us
    dot_general x4, matrix products, pick_rows(): jnp.dot(selection, flattened, preferred_element_type=jnp.float32)  10.7 us
    all_to_all x1, starting transfers between devices, local(): lax.all_to_all(outgoing_keys, 'replica', split_axis=0, concat_axis=0, til...  7.86 us
  transfers between devices with their start and end apart: 2, of which 1 were waited for; matrix products, arithmetic and copies ran while one was open for 13% of the time, Pallas kernels for 0%

commit v1 on v0

--- a/solution.py
+++ b/solution.py
@@ -29,32 +29,23 @@
     ) * HEAD_DIM ** (-0.5)
 
 
-def finish(queries, own_part, block_vals, past_keys, past_vals, live):
-    past_part = jnp.einsum(
-        "sqhd,skhd->shqk",
-        split_heads(queries),
-        split_heads(past_keys),
+def partial(scores, vals):
+    row_max = jnp.max(scores, axis=-1, keepdims=True)
+    weights = jnp.exp(scores - row_max)
+    total = jnp.sum(weights, axis=-1, keepdims=True)
+    result = jnp.einsum(
+        "shqk,skhd->sqhd",
+        (weights / total).astype(jnp.bfloat16),
+        split_heads(vals),
         preferred_element_type=jnp.float32,
-    ) * HEAD_DIM ** (-0.5)
-    valid = jnp.arange(past_keys.shape[1], dtype=jnp.int32)[None, :] < live[:, None]
-    past_part = jnp.where(valid[:, None, None, :], past_part, -1e30)
-    row_max = jnp.maximum(
-        jnp.max(past_part, axis=-1, keepdims=True), jnp.max(own_part, axis=-1, keepdims=True)
     )
-    past_exp = jnp.exp(past_part - row_max)
-    own_exp = jnp.exp(own_part - row_max)
-    denominator = jnp.sum(past_exp, axis=-1, keepdims=True) + jnp.sum(
-        own_exp, axis=-1, keepdims=True
-    )
-    past_weights = (past_exp / denominator).astype(jnp.bfloat16)
-    own_weights = (own_exp / denominator).astype(jnp.bfloat16)
-    result = jnp.einsum(
-        "shqk,skhd->sqhd", past_weights, split_heads(past_vals), preferred_element_type=jnp.float32
-    )
-    result = result + jnp.einsum(
-        "shqk,skhd->sqhd", own_weights, split_heads(block_vals), preferred_element_type=jnp.float32
-    )
-    return result.reshape(queries.shape).astype(jnp.bfloat16)
+    return result, (row_max + jnp.log(total))[..., 0]
+
+
+def pick_exact(selection, rows):
+    flattened = rows.reshape(rows.shape[0], -1)
+    picked = jnp.dot(selection.astype(jnp.float32), flattened, precision=lax.Precision.HIGHEST)
+    return picked.reshape((selection.shape[0],) + rows.shape[1:])
 
 
 def local(
@@ -98,10 +89,7 @@
     send_select = ((dest_local * capacity + rank_local)[None, :] == bucket_ids[:, None]).astype(
         jnp.bfloat16
     )
-    all_slots, all_lengths = (
-        lax.all_gather(new_slot, "replica", axis=0, tiled=True),
-        lax.all_gather(lengths, "replica", axis=0, tiled=True),
-    )
+    all_slots = lax.all_gather(new_slot, "replica", axis=0, tiled=True)
     stream_total = all_slots.shape[0]
     dest_board = (all_slots // slot_count).reshape(peer_count, slot_count)
     matches = (dest_board[:, None, :] == dest_board[:, :, None]) & (
@@ -115,19 +103,25 @@
         (column[:, None] == bucket_ids[None, :]).astype(jnp.float32),
         preferred_element_type=jnp.float32,
     ).astype(jnp.bfloat16)
-    live_new = jnp.dot(
-        arrive, all_lengths.astype(jnp.float32), preferred_element_type=jnp.float32
-    ).astype(jnp.int32)
-    own_part = own_scores(query_normed, key_normed)
-    outgoing_keys = pick_rows(send_select, cache_keys)
-    outgoing_values = pick_rows(send_select, cache_values)
-    arrived_keys, arrived_values = (
-        lax.all_to_all(outgoing_keys, "replica", split_axis=0, concat_axis=0, tiled=True),
-        lax.all_to_all(outgoing_values, "replica", split_axis=0, concat_axis=0, tiled=True),
+    outgoing = pick_rows(receive_select.T, query_normed)
+    arrived = lax.all_to_all(outgoing, "replica", split_axis=0, concat_axis=0, tiled=True)
+    own_result, own_level = partial(own_scores(query_normed, key_normed), block_values)
+    visitors = pick_rows(send_select.T, arrived)
+    past_part = own_scores(visitors, cache_keys)
+    valid = jnp.arange(cache_keys.shape[1], dtype=jnp.int32)[None, :] < lengths[:, None]
+    past_part = jnp.where(valid[:, None, None, :], past_part, -1e30)
+    past_result, past_level = partial(past_part, cache_values)
+    past_result = past_result.astype(jnp.bfloat16).reshape(query_raw.shape)
+    sent_result, sent_level = pick_rows(send_select, past_result), pick_exact(send_select, past_level)
+    back_result, back_level = (
+        lax.all_to_all(sent_result, "replica", split_axis=0, concat_axis=0, tiled=True),
+        lax.all_to_all(sent_level, "replica", split_axis=0, concat_axis=0, tiled=True),
     )
-    moved_keys = pick_rows(receive_select, arrived_keys)
-    moved_values = pick_rows(receive_select, arrived_values)
-    return finish(query_normed, own_part, block_values, moved_keys, moved_values, live_new)
+    past_result = split_heads(pick_rows(receive_select, back_result)).astype(jnp.float32)
+    past_level = pick_exact(receive_select, back_level)
+    share = jax.nn.sigmoid(past_level - own_level).transpose(0, 2, 1)[..., None]
+    result = own_result + share * (past_result - own_result)
+    return result.reshape(query_raw.shape).astype(jnp.bfloat16)
 
 
 def solution(mesh):

time: 315 us -> 133 us (0.42); the launches traced: 309 us -> 132 us
  blocking collectives: 117 us -> 16.4 us
  waiting for transfers between devices: 105 us -> 44.4 us
  local copies, waits for them, and re-layouts: 46.1 us -> 31.9 us
  matrix products: 23 us -> 18.4 us
    unnamed x1, blocking collectives: 113 us -> 13.1 us
    all_to_all x2 -> x3, waiting for transfers between devices: 105 us -> 44.4 us  [the longest x1 25.2 us: local(): lax.all_to_all(sent_result, 'replica', split_axis=0, concat_axis=0, tiled...]
    another operation x2 -> x1, local copies, waits for them, and re-layouts: 14 us -> 1.85 us  [split_heads(): source_rows.reshape(source_rows.shape[0], source_rows.shape[1], source_ro...]
    unnamed x33 -> x31, local copies, waits for them, and re-layouts: 30.7 us -> 22 us
    dot_general x4, matrix products: 10.7 us -> 4.89 us  [pick_rows(): jnp.dot(selection, flattened, preferred_element_type=jnp.float32)]
    convert_element_type x1 -> x3, local copies, waits for them, and re-layouts: 1.12 us -> 5.03 us  [the longest x1 3.44 us: local(): split_heads(pick_rows(receive_select, back_result)).astype(jnp.float32)]
    dot_general x1 -> x2, matrix products: 2.2 us -> 5.9 us  [own_scores(): jnp.einsum('sqhd,skhd->shqk', split_heads(queries), split_heads(block_key...]
    all_to_all x2 -> x3, starting transfers between devices: 12.6 us -> 13.3 us  [the longest x1 6.13 us: local(): lax.all_to_all(sent_result, 'replica', split_axis=0, concat_axis=0, tiled...]
  transfers between devices with their start and end apart: 2 -> 3, of which waited for: 1 -> 2; matrix products, arithmetic and copies ran while one was open for 13% -> 20% of each run, Pallas kernels for 0% -> 0%
where the time goes in v1:
time: 133 us; the launch traced here: 132 us
  waiting for transfers between devices  44.4 us (33%)
  local copies, waits for them, and re-layouts  31.9 us (24%)
  matrix products  18.4 us (14%)
  blocking collectives  16.4 us (12%)
  starting transfers between devices  13.3 us (10%)
  other arithmetic  6.53 us (5%)
    all_to_all x1, waiting for transfers between devices, local(): lax.all_to_all(sent_result, 'replica', split_axis=0, concat_axis=0, tiled...  25.2 us
    unnamed x31, local copies, waits for them, and re-layouts  22 us
    all_to_all x1, waiting for transfers between devices, local(): lax.all_to_all(outgoing, 'replica', split_axis=0, concat_axis=0, tiled=True)  19.2 us
    unnamed x1, blocking collectives  13.1 us
    dot_general x2, matrix products, partial(): jnp.einsum('shqk,skhd->sqhd', (weights / total).astype(jnp.bfloat16), spl...  7.06 us
    all_to_all x1, starting transfers between devices, local(): lax.all_to_all(sent_result, 'replica', split_axis=0, concat_axis=0, tiled...  6.13 us
    dot_general x2, matrix products, own_scores(): jnp.einsum('sqhd,skhd->shqk', split_heads(queries), split_heads(block_key...  5.9 us
    dot_general x4, matrix products, pick_rows(): jnp.dot(selection, flattened, preferred_element_type=jnp.float32)  4.89 us
  transfers between devices with their start and end apart: 3, of which 2 were waited for; matrix products, arithmetic and copies ran while one was open for 20% of the time, Pallas kernels for 0%

profile of v1, /device:TPU:0, one launch (start us, length us, event | category | flops | bytes accessed | tf_op | source)
XLA Modules:
  0.0 131.9 jit_solution(11853902153606377783)
XLA Ops:
  0.0 1.4 %dynamic-slice = u32[1]{0:T(128)} dynamic-slice(u32[32]{0:T(128)} %constant.55, u32[]{:T(128)S(6)} %add.74), dynamic_slice_sizes={1} | dynamic-slice | bytes 12
  2.1 0.9 dynamic-update-slice
  2.9 13.1 %all-reduce = s32[96]{0:T(128)S(1)} all-reduce(s32[96]{0:T(128)S(1)} %dynamic-update-slice), channel_id=1, replica_groups=mesh['groups'=2,'replica'=8,'tensor'=2] {'replica'}, use_global_device_ids=true, to_apply=%add | all-reduce | flops 96 | bytes 768
  16.7 1.5 %fusion.1 = f32[12,32]{1,0:T(8,128)S(1)} fusion(bf16[12,32,1280]{2,1,0:T(8,128)(2,1)} %param.13), kind=kLoop, calls=%fused_computation.9 | loop fusion | flops 1474176 | bytes 984576 | tf_op jit(solution)/shard_map/reduce_sum | solution.py:71
  18.2 1.5 %fusion.4 = f32[12,32]{1,0:T(8,128)S(1)} fusion(bf16[12,32,1280]{2,1,0:T(8,128)(2,1)} %param.14), kind=kLoop, calls=%fused_computation.12 | loop fusion | flops 1474176 | bytes 984576 | tf_op jit(solution)/shard_map/reduce_sum | solution.py:71
  19.7 3.3 %all-reduce.1 = (f32[12,32]{1,0:T(8,128)S(1)}, f32[12,32]{1,0:T(8,128)S(1)}) all-reduce(f32[12,32]{1,0:T(8,128)S(1)} %fusion.1, f32[12,32]{1,0:T(8,128)S(1)} %fusion.4), channel_id=1, replica_groups=mesh['groups'=2,'replica'=8,'tensor'=2] {'tensor'}, use_global_device_ids=true, to_apply=%region_1.0 | all-reduce | flops 768 | bytes 6144 | tf_op jit(solution)/shard_map/psum | solution.py:70
  23.4 0.7 copy.83
  24.9 1.4 %copy.84 = bf16[2,8,32,1280]{3,2,1,0:T(8,128)(2,1)} copy(bf16[2,8,32,1280]{3,1,2,0:T(8,128)(2,1)S(1)} %bitcast.87) | data formatting | bytes 2621440
  26.3 3.6 %all-to-all-start = ((bf16[16,32,1280]{2,1,0:T(8,128)(2,1)}), bf16[16,32,1280]{2,1,0:T(8,128)(2,1)S(1)}, u32[]{:S(2)}, u32[]{:S(2)}) async-start(bf16[16,32,1280]{2,1,0:T(8,128)(2,1)} %bitcast.82), calls=%async_computation | async-start | bytes 2621440 | tf_op jit(solution)/shard_map/all_to_all | solution.py:107
  29.9 6.3 %copy.62 = bf16[12,128,1280]{1,2,0:T(8,128)(2,1)} copy(bf16[12,128,1280]{2,1,0:T(8,128)(2,1)} %param.9) | data formatting | bytes 7864320 | tf_op args[0]
  36.2 6.3 %copy.71 = bf16[12,128,1280]{1,2,0:T(8,128)(2,1)} copy(bf16[12,128,1280]{2,1,0:T(8,128)(2,1)} %param.10) | data formatting | bytes 7864320 | tf_op args[1]
  42.8 19.2 %all-to-all-done = bf16[16,32,1280]{2,1,0:T(8,128)(2,1)S(1)} async-done(((bf16[16,32,1280]{2,1,0:T(8,128)(2,1)}), bf16[16,32,1280]{2,1,0:T(8,128)(2,1)S(1)}, u32[]{:S(2)}, u32[]{:S(2)}) %all-to-all-start) | async-done | bytes 1310752 | tf_op jit(solution)/shard_map/all_to_all | solution.py:107
  62.0 0.7 copy.85
  63.2 1.9 %reshape_reshape.7 = bf16[12,32,10,128]{3,2,1,0:T(8,128)(2,1)} reshape(bf16[12,40960]{1,0:T(8,128)(2,1)S(1)} %convolution_convert_fusion.2) | data formatting | bytes 1966080 | tf_op jit(solution)/shard_map/reshape;reshape | solution.py:10
  65.1 3.8 %fusion.9 = (f32[12,10,32]{2,1,0:T(8,128)S(1)}, f32[12,10,32,128]{3,2,1,0:T(8,128)S(1)}) fusion(pred[12,128]{1,0:T(8,128)(4,1)S(1)} %iota_compare_fusion.2, bf16[12,128,10,128]{1,3,2,0:T(8,128)(2,1)} %bitcast.79, bf16[12,32,10,128]{3,2,1,0:T(8,128)(2,1)} %reshape_reshape.7), kind=kOutput, calls=%fused_computation.25 | convolution fusion | flops 127299840 | bytes 6898176 | tf_op jit(solution)/shard_map/sqhd,skhd->shqk/dot_general | solution.py:24
  68.9 1.2 fusion.11
  70.6 0.7 reshape.147
  71.3 3.6 %all-to-all-start.1 = ((f32[8,1,640]{2,1,0:T(1,128)}), f32[8,1,640]{2,1,0:T(1,128)S(1)}, u32[]{:S(2)}, u32[]{:S(2)}) async-start(f32[8,1,640]{2,1,0:T(1,128)} %reshape.147), calls=%async_computation.1 | async-start | bytes 40960 | tf_op jit(solution)/shard_map/all_to_all | solution.py:118
  74.9 3.9 %fusion.12 = bf16[12,32,10,128]{3,1,2,0:T(8,128)(2,1)S(1)} fusion(bf16[12,128,10,128]{1,3,2,0:T(8,128)(2,1)} %bitcast.89, f32[12,10,32,128]{3,2,1,0:T(8,128)S(1)} %get-tuple-element.8, f32[12,10,32]{2,1,0:T(8,128)S(1)} %fusion.11, f32[12,10,32]{2,1,0:T(8,128)S(1)} %get-tuple-element.7, pred[12,128]{1,0:T(8,128)(4,1)S(1)} %iota_compare_fusion.2), kind=kOutput, calls=%fused_computation.29 | convolution fusion | flops 128778240 | bytes 6913536 | tf_op jit(solution)/shard_map/shqk,skhd->sqhd/dot_general | solution.py:36
  79.3 1.8 %reshape_reshape.8 = bf16[12,40960]{1,0:T(8,128)(2,1)} reshape(bf16[12,32,10,128]{3,2,1,0:T(8,128)(2,1)S(1)} %copy.73) | data formatting | bytes 1966080 | tf_op jit(solution)/shard_map/reshape;reshape | solution.py:16
  81.1 1.8 %convolution_convert_fusion.1 = bf16[16,40960]{1,0:T(8,128)(2,1)S(1)} fusion(bf16[12,40960]{1,0:T(8,128)(2,1)} %reshape_reshape.8, s32[12]{0:T(128)S(1)} %multiply_add_fusion), kind=kOutput, calls=%fused_computation.2 | convolution fusion | flops 16384192 | bytes 2293808 | tf_op jit(solution)/shard_map/dot_general | solution.py:17
  82.9 1.3 %copy.86 = bf16[2,8,32,1280]{3,2,1,0:T(8,128)(2,1)} copy(bf16[2,8,32,1280]{3,1,2,0:T(8,128)(2,1)S(1)} %bitcast.85) | data formatting | bytes 2621440
  84.3 6.1 %all-to-all-start.2 = ((bf16[16,32,1280]{2,1,0:T(8,128)(2,1)}), bf16[16,32,1280]{2,1,0:T(8,128)(2,1)S(1)}, u32[]{:S(2)}, u32[]{:S(2)}) async-start(bf16[16,32,1280]{2,1,0:T(8,128)(2,1)} %bitcast.28), calls=%async_computation.2 | async-start | bytes 2621440 | tf_op jit(solution)/shard_map/all_to_all | solution.py:117
  90.4 2.1 %multiply_reduce_fusion = (f32[12,10,32]{2,1,0:T(8,128)S(1)}, f32[12,10,32,32]{2,3,1,0:T(8,128)S(1)}) fusion(f32[1280]{0:T(1024)S(1)} %convert_element_type.69, f32[12,32]{1,0:T(8,128)S(1)} %get-tuple-element.12, bf16[12,32,1280]{2,1,0:T(8,128)(2,1)S(1)} %copy-done.2, bf16[12,32,1280]{2,1,0:T(8,128)(2,1)} %param.14, f32[1280]{0:T(1024)S(1)} %convert_element_type.72, ...), kind=kOutput, calls=%fused_computation.24 | convolution fusion | flops 35631360 | bytes 2486272 | tf_op jit(solution)/shard_map/sqhd,skhd->shqk/dot_general | solution.py:24
  92.5 1.3 copy-done.3
  95.0 0.7 reduce
  96.2 25.2 %all-to-all-done.2 = bf16[16,32,1280]{2,1,0:T(8,128)(2,1)S(1)} async-done(((bf16[16,32,1280]{2,1,0:T(8,128)(2,1)}), bf16[16,32,1280]{2,1,0:T(8,128)(2,1)S(1)}, u32[]{:S(2)}, u32[]{:S(2)}) %all-to-all-start.2) | async-done | bytes 1310752 | tf_op jit(solution)/shard_map/all_to_all | solution.py:117
  121.4 0.7 copy.87
  122.2 2.0 %fusion = f32[12,40960]{1,0:T(8,128)} fusion(bf16[12,16]{1,0:T(8,128)(2,1)S(1)} %convolution_convert_fusion.5, bf16[16,40960]{1,0:T(8,128)(2,1)S(1)} %bitcast.86), kind=kOutput, calls=%fused_computation.1 | convolution fusion | flops 16711680 | bytes 3277184 | tf_op jit(solution)/shard_map/dot_general | solution.py:17
  124.2 3.4 %reshape.139 = f32[12,32,10,128]{3,2,1,0:T(8,128)} reshape(f32[12,40960]{1,0:T(8,128)} %fusion) | data formatting | bytes 3932160 | tf_op jit(solution)/shard_map/convert_element_type | solution.py:120
  127.6 3.1 %fusion.13 = bf16[12,10,4,8,128]{4,3,2,1,0:T(8,128)(2,1)S(1)} fusion(f32[12,32,10,128]{3,2,1,0:T(8,128)} %reshape.139, f32[12,32,10]{1,2,0:T(8,128)S(1)} %copy.70, f32[12,10,32,32]{2,3,1,0:T(8,128)S(1)} %copy-done.4, f32[12,10,32]{2,1,0:T(8,128)S(1)} %fusion.10, f32[12,10,32]{2,1,0:T(8,128)S(1)} %get-tuple-element.9, bf16[12,32,1280]{2,1,0:T(8,128)(2,1)S(1)} %copy-done), kind=kOutput, calls=%fused_computation.30 | convolution fusion | flops 33914880 | bytes 4469760 | tf_op jit(solution)/shard_map/shqk,skhd->sqhd/dot_general | solution.py:36
  130.8 1.1 copy.122
  (53 shorter events, 5.2 us)
Async XLA Ops:
  0.0 127.6 %copy-start = (bf16[12,32,1280]{2,1,0:T(8,128)(2,1)S(1)}, bf16[12,32,1280]{2,1,0:T(8,128)(2,1)}, u32[]{:S(2)}) copy-start(bf16[12,32,1280]{2,1,0:T(8,128)(2,1)} %param.15) | copy-start | bytes 2949124
  0.0 23.0 %copy-start.1 = (bf16[12,32,1280]{2,1,0:T(8,128)(2,1)S(1)}, bf16[12,32,1280]{2,1,0:T(8,128)(2,1)}, u32[]{:S(2)}) copy-start(bf16[12,32,1280]{2,1,0:T(8,128)(2,1)} %param.13) | copy-start | bytes 2949124
  0.0 19.7 %copy-start.5 = (bf16[1280]{0:T(1024)(128)(2,1)S(1)}, bf16[1280]{0:T(1024)(128)(2,1)}, u32[]{:S(2)}) copy-start(bf16[1280]{0:T(1024)(128)(2,1)} %param.16) | copy-start | bytes 7684
  26.3 35.7 %all-to-all-start = ((bf16[16,32,1280]{2,1,0:T(8,128)(2,1)}), bf16[16,32,1280]{2,1,0:T(8,128)(2,1)S(1)}, u32[]{:S(2)}, u32[]{:S(2)}) async-start(bf16[16,32,1280]{2,1,0:T(8,128)(2,1)} %bitcast.82), calls=%async_computation | async-start | bytes 2621440 | tf_op jit(solution)/shard_map/all_to_all | solution.py:107
  36.2 6.3 %copy-start.8 = (s32[12]{0:T(128)S(1)}, s32[12]{0:T(128)}, u32[]{:S(2)}) copy-start(s32[12]{0:T(128)} %param.12) | copy-start | bytes 148
  36.2 6.5 %copy-start.7 = (s32[12]{0:T(128)S(1)}, s32[12]{0:T(128)}, u32[]{:S(2)}) copy-start(s32[12]{0:T(128)} %param.11) | copy-start | bytes 148
  71.3 13.0 %all-to-all-start.1 = ((f32[8,1,640]{2,1,0:T(1,128)}), f32[8,1,640]{2,1,0:T(1,128)S(1)}, u32[]{:S(2)}, u32[]{:S(2)}) async-start(f32[8,1,640]{2,1,0:T(1,128)} %reshape.147), calls=%async_computation.1 | async-start | bytes 40960 | tf_op jit(solution)/shard_map/all_to_all | solution.py:118
  84.3 6.1 %copy-start.6 = (bf16[1280]{0:T(1024)(128)(2,1)S(1)}, bf16[1280]{0:T(1024)(128)(2,1)}, u32[]{:S(2)}) copy-start(bf16[1280]{0:T(1024)(128)(2,1)} %param.17) | copy-start | bytes 7684
  84.3 6.2 %copy-start.2 = (bf16[12,32,1280]{2,1,0:T(8,128)(2,1)S(1)}, bf16[12,32,1280]{2,1,0:T(8,128)(2,1)}, u32[]{:S(2)}) copy-start(bf16[12,32,1280]{2,1,0:T(8,128)(2,1)} %param.13) | copy-start | bytes 2949124
  84.3 37.2 %all-to-all-start.2 = ((bf16[16,32,1280]{2,1,0:T(8,128)(2,1)}), bf16[16,32,1280]{2,1,0:T(8,128)(2,1)S(1)}, u32[]{:S(2)}, u32[]{:S(2)}) async-start(bf16[16,32,1280]{2,1,0:T(8,128)(2,1)} %bitcast.28), calls=%async_computation.2 | async-start | bytes 2621440 | tf_op jit(solution)/shard_map/all_to_all | solution.py:117
  92.5 1.3 copy-start.3
  124.2 3.5 %copy-start.4 = (f32[12,10,32,32]{2,3,1,0:T(8,128)S(1)}, f32[12,10,32,32]{2,3,1,0:T(8,128)}, u32[]{:S(2)}) copy-start(f32[12,10,32,32]{2,3,1,0:T(8,128)} %copy-done.3) | copy-start | bytes 1474564

commit v2 on v1

v2 whole, which is shorter than its diff:
```python
import functools

import jax
import jax.numpy as jnp
from jax import lax
from jax.experimental import pallas as pl
from jax.experimental.pallas import tpu as pltpu
from jax.sharding import PartitionSpec as P

HEAD_DIM = 128
PAIR = 2 * HEAD_DIM
LANES = 128
MESH = pl.DeviceIdType.MESH
F32 = jnp.float32
BF16 = jnp.bfloat16


def pair_attention(queries, keys, values, valid):
    rows = queries.shape[0]
    zeros = jnp.zeros((rows, HEAD_DIM), queries.dtype)
    diagonal = jnp.concatenate(
        [
            jnp.concatenate([queries[:, :HEAD_DIM], zeros], axis=1),
            jnp.concatenate([zeros, queries[:, HEAD_DIM:]], axis=1),
        ],
        axis=0,
    )
    scores = lax.dot_general(
        diagonal, keys, (((1,), (1,)), ((), ())), preferred_element_type=F32
    ) * HEAD_DIM ** (-0.5)
    if valid is not None:
        scores = jnp.where(valid, scores, -1e30)
    top = jnp.max(scores, axis=1, keepdims=True)
    weights = jnp.exp(scores - top)
    total = jnp.sum(weights, axis=1, keepdims=True)
    result = jnp.dot(weights.astype(BF16), values, preferred_element_type=F32)
    inverse = 1.0 / total
    first = result[:rows, :HEAD_DIM] * inverse[:rows]
    second = result[rows:, HEAD_DIM:] * inverse[rows:]
    level = top + jnp.log(total)
    return jnp.concatenate([first, second], axis=1), level[:rows], level[rows:]


def kernel(
    peers,
    capacity,
    full_width,
    row_ref,
    lengths_ref,
    query_hbm,
    key_hbm,
    value_hbm,
    cache_key_hbm,
    cache_value_hbm,
    query_gain_ref,
    key_gain_ref,
    out_ref,
    query,
    key,
    value,
    cache_key,
    cache_value,
    squares,
    squares_other,
    tables,
    picks_vmem,
    picks,
    query_out,
    query_in,
    result_out,
    result_in,
    own_result,
    own_level,
    load_sem,
    square_sem,
    table_send,
    table_recv,
    query_send,
    query_recv,
    result_send,
    result_recv,
):
    slots, block, width = query.shape
    pairs = width // PAIR
    me = lax.axis_index("replica")
    other = 1 - lax.axis_index("tensor")

    def peer(d):
        return lax.rem(me + d, peers)

    def order(k):
        half = (k + 1) // 2
        return jnp.where(lax.rem(k, 2) == 0, peers // 2 + half, peers // 2 - half)

    loads = [
        pltpu.make_async_copy(source, target, load_sem.at[n])
        for n, (source, target) in enumerate(
            (
                (query_hbm, query),
                (key_hbm, key),
                (value_hbm, value),
                (cache_key_hbm, cache_key),
                (cache_value_hbm, cache_value),
            )
        )
    ]
    for load in loads:
        load.start()

    barrier = pltpu.get_barrier_semaphore()
    pl.semaphore_signal(barrier, inc=1, device_id={"tensor": other}, device_id_type=MESH)

    def greet(d, carry):
        pl.semaphore_signal(barrier, inc=1, device_id={"replica": peer(d)}, device_id_type=MESH)
        return carry

    lax.fori_loop(1, peers, greet, 0)
    tables[0] = row_ref[...]
    pl.semaphore_wait(barrier, peers)

    def table_copy(d):
        return pltpu.make_async_remote_copy(
            src_ref=row_ref,
            dst_ref=tables.at[d],
            send_sem=table_send.at[d],
            recv_sem=table_recv.at[d],
            device_id={"replica": peer(d)},
            device_id_type=MESH,
        )

    lax.fori_loop(1, peers, lambda d, carry: (table_copy(d).start(), carry)[1], 0)

    lane = lax.broadcasted_iota(jnp.int32, (block, LANES), 1)
    sums = jnp.zeros((block, LANES), F32)
    for ref, load, offset in ((query, loads[0], 0), (key, loads[1], LANES // 2)):
        load.wait()
        for i in range(slots):
            rows = ref[i].astype(F32)
            total = jnp.sum(rows * rows, axis=1, keepdims=True)
            sums = jnp.where(lane == offset + i, total, sums)
    squares[...] = sums
    exchange = pltpu.make_async_remote_copy(
        src_ref=squares,
        dst_ref=squares_other,
        send_sem=square_sem.at[0],
        recv_sem=square_sem.at[1],
        device_id={"tensor": other},
        device_id_type=MESH,
    )
    exchange.start()

    lax.fori_loop(1, peers, lambda d, carry: (table_copy(d).wait_recv(), carry)[1], 0)
    board = tables[:, 0, :]
    shape = board.shape
    column = lax.broadcasted_iota(jnp.int32, shape, 1)
    sender = lax.broadcasted_iota(jnp.int32, shape, 0)
    mirrored = jnp.where(sender == 0, 0, peers - sender)
    own_row = jnp.broadcast_to(tables[0][0:1], shape)
    back_base = lax.rem(me - sender + peers, peers) * slots
    chosen = jnp.zeros(shape, jnp.int32)
    places = jnp.zeros(shape, jnp.int32)
    mine = (board >= me * slots) & (board < me * slots + slots)
    theirs = (own_row >= back_base) & (own_row < back_base + slots)
    for r in range(capacity):
        first = jnp.min(jnp.where(mine, column, LANES), axis=1, keepdims=True)
        now = mine & (column == first)
        local = jnp.max(jnp.where(now, board - me * slots, 0), axis=1, keepdims=True)
        chosen = jnp.where(column == r, local, chosen)
        places = jnp.where(now, mirrored * capacity + r, places)
        mine = mine & (column != first)
        first = jnp.min(jnp.where(theirs, column, LANES), axis=1, keepdims=True)
        chosen = jnp.where(column == capacity + r, jnp.where(first == LANES, 0, first), chosen)
        theirs = theirs & (column != first)
    for i in range(slots):
        matching = jnp.where(board == me * slots + i, places, 0)
        place = jnp.max(jnp.max(matching, axis=1, keepdims=True), axis=0, keepdims=True)
        chosen = jnp.where(column == 2 * capacity + i, place, chosen)
    picks_vmem[...] = chosen
    to_scalars = pltpu.make_async_copy(picks_vmem, picks, load_sem.at[5])
    to_scalars.start()

    exchange.wait()
    factors = lax.rsqrt((squares[...] + squares_other[...]) / full_width + 1e-06)
    for i in range(slots):
        query[i] = (
            query[i].astype(F32) * factors[:, i : i + 1] * query_gain_ref[...].astype(F32)
        ).astype(BF16)
    to_scalars.wait()

    def query_copy(d):
        return pltpu.make_async_remote_copy(
            src_ref=query_out.at[d],
            dst_ref=query_in.at[d],
            send_sem=query_send.at[d],
            recv_sem=query_recv.at[d],
            device_id={"replica": peer(d)},
            device_id_type=MESH,
        )

    def result_copy(d):
        return pltpu.make_async_remote_copy(
            src_ref=result_out.at[d],
            dst_ref=result_in.at[d],
            send_sem=result_send.at[d],
            recv_sem=result_recv.at[d],
            device_id={"replica": lax.rem(me - d + peers, peers)},
            device_id_type=MESH,
        )

    def send_queries(k, carry):
        d = order(k)
        for r in range(capacity):
            query_out[d, r] = query[picks[peers - d, r]]
        query_copy(d).start()
        return carry

    lax.fori_loop(0, peers - 1, send_queries, 0)

    cached = cache_key.shape[1]
    position = lax.broadcasted_iota(jnp.int32, (2 * block, cached), 1)

    def visit(d, r, fetch, target):
        g = picks[d, capacity + r]
        valid = position < lengths_ref[g]
        levels = jnp.zeros((block, LANES), F32)
        for c in range(pairs):
            part = slice(c * PAIR, (c + 1) * PAIR)
            result, even, odd = pair_attention(
                fetch(part), cache_key[g, :, part], cache_value[g, :, part], valid
            )
            target[d, r, :, part] = result.astype(BF16)
            levels = jnp.where(lane % 32 == 2 * c, even, levels)
            levels = jnp.where(lane % 32 == 2 * c + 1, odd, levels)
        high = levels.astype(BF16).astype(F32)
        middle = (levels - high).astype(BF16).astype(F32)
        low = levels - high - middle
        pieces = jnp.where(lane < 32, high, jnp.where(lane < 64, middle, low))
        target[d, r, :, width:] = pieces.astype(BF16)

    def own_block(i, carry):
        levels = jnp.zeros((block, LANES), F32)
        for c in range(pairs):
            part = slice(c * PAIR, (c + 1) * PAIR)
            result, even, odd = pair_attention(
                query[i, :, part], key[i, :, part], value[i, :, part], None
            )
            own_result[i, :, part] = result
            levels = jnp.where(lane == 2 * c, even, levels)
            levels = jnp.where(lane == 2 * c + 1, odd, levels)
        own_level[i] = levels
        return carry

    for i in range(slots):
        at = LANES // 2 + i
        key[i] = (
            key[i].astype(F32) * factors[:, at : at + 1] * key_gain_ref[...].astype(F32)
        ).astype(BF16)
    for load in loads[2:]:
        load.wait()
    for r in range(capacity):
        i = picks[0, r]
        visit(0, r, lambda part: query[i, :, part], result_in)
    lax.fori_loop(0, slots, own_block, 0)

    def serve(k, carry):
        d = order(k)
        query_copy(d).wait_recv()
        for r in range(capacity):
            visit(d, r, lambda part: query_in[d, r, :, part], result_out)
        result_copy(d).start()
        return carry

    lax.fori_loop(0, peers - 1, serve, 0)
    lax.fori_loop(1, peers, lambda d, carry: (result_copy(d).wait_recv(), carry)[1], 0)

    def combine(i, carry):
        at = picks[0, 2 * capacity + i]
        from_peer, r = at // capacity, lax.rem(at, capacity)
        pieces = result_in[from_peer, r, :, width:].astype(F32)
        level = pieces + pltpu.roll(pieces, LANES - 32, 1) + pltpu.roll(pieces, LANES - 64, 1)
        share = 1.0 / (1.0 + jnp.exp(own_level[i] - level))
        for h in range(width // HEAD_DIM):
            part = slice(h * HEAD_DIM, (h + 1) * HEAD_DIM)
            own = own_result[i, :, part]
            past = result_in[from_peer, r, :, part].astype(F32)
            out_ref[i, :, part] = (own + share[:, h : h + 1] * (past - own)).astype(BF16)
        return carry

    lax.fori_loop(0, slots, combine, 0)

    def finish_sends(d, carry):
        table_copy(d).wait_send()
        query_copy(d).wait_send()
        result_copy(d).wait_send()
        return carry

    lax.fori_loop(1, peers, finish_sends, 0)


def local(
    cache_keys,
    cache_values,
    lengths,
    new_slot,
    query_raw,
    block_keys_raw,
    block_values,
    query_gain,
    key_gain,
):
    slots, block, width = query_raw.shape
    cached = cache_keys.shape[1]
    peers = lax.axis_size("replica")
    capacity = -(-slots // peers)
    full_width = width * lax.axis_size("tensor")
    row = jnp.broadcast_to(
        jnp.pad(new_slot, (0, LANES - slots), constant_values=-1)[None], (8, LANES)
    )
    vmem = pl.BlockSpec(memory_space=pltpu.VMEM)
    smem = pl.BlockSpec(memory_space=pltpu.SMEM)
    hbm = pl.BlockSpec(memory_space=pl.ANY)
    message = (peers, capacity, block, width)
    answer = (peers, capacity, block, width + LANES)
    dma = pltpu.SemaphoreType.DMA
    return pl.pallas_call(
        functools.partial(kernel, peers, capacity, full_width),
        out_shape=jax.ShapeDtypeStruct(query_raw.shape, BF16),
        in_specs=[vmem, smem, hbm, hbm, hbm, hbm, hbm, vmem, vmem],
        out_specs=vmem,
        scratch_shapes=[
            pltpu.VMEM(query_raw.shape, BF16),
            pltpu.VMEM(query_raw.shape, BF16),
            pltpu.VMEM(query_raw.shape, BF16),
            pltpu.VMEM(cache_keys.shape, BF16),
            pltpu.VMEM(cache_keys.shape, BF16),
            pltpu.VMEM((block, LANES), F32),
            pltpu.VMEM((block, LANES), F32),
            pltpu.VMEM((peers, 8, LANES), jnp.int32),
            pltpu.VMEM((peers, LANES), jnp.int32),
            pltpu.SMEM((peers, LANES), jnp.int32),
            pltpu.VMEM(message, BF16),
            pltpu.VMEM(message, BF16),
            pltpu.VMEM(answer, BF16),
            pltpu.VMEM(answer, BF16),
            pltpu.VMEM(query_raw.shape, F32),
            pltpu.VMEM((slots, block, LANES), F32),
            dma((6,)),
            dma((2,)),
            dma((peers,)),
            dma((peers,)),
            dma((peers,)),
            dma((peers,)),
            dma((peers,)),
            dma((peers,)),
        ],
        compiler_params=pltpu.CompilerParams(
            collective_id=0, has_side_effects=True, vmem_limit_bytes=48 * 1024 * 1024
        ),
        cost_estimate=pl.CostEstimate(
            flops=4 * slots * block * (cached + block) * width,
            bytes_accessed=4 * cache_keys.size + 8 * query_raw.size,
            transcendentals=slots * block * (cached + block) * width // HEAD_DIM,
        ),
    )(
        row,
        lengths,
        query_raw,
        block_keys_raw,
        block_values,
        cache_keys,
        cache_values,
        query_gain[None],
        key_gain[None],
    )


def solution(mesh):
    in_specs = (
        P(("groups", "replica"), None, "tensor"),
        P(("groups", "replica"), None, "tensor"),
        P(("groups", "replica")),
        P(("groups", "replica")),
        P(("groups", "replica"), None, "tensor"),
        P(("groups", "replica"), None, "tensor"),
        P(("groups", "replica"), None, "tensor"),
        P("tensor"),
        P("tensor"),
    )
    out_specs = P(("groups", "replica"), None, "tensor")
    return jax.shard_map(local, mesh=mesh, in_specs=in_specs, out_specs=out_specs, check_vma=False)
```

time: 133 us -> 83.4 us (0.63)
  Pallas kernels: 0 us -> 75.8 us
  waiting for transfers between devices: 44.4 us -> 0 us
  local copies, waits for them, and re-layouts: 31.9 us -> 7.25 us
  matrix products: 18.4 us -> 0 us
  blocking collectives: 16.4 us -> 0 us
  starting transfers between devices: 13.3 us -> 0 us
  other arithmetic: 6.53 us -> 0 us
    pallas_call x0 -> x1, Pallas kernels: none -> 75.8 us  [local(): pl.pallas_call(functools.partial(kernel, peers, capacity, full_width), ou...]
    all_to_all x3 -> x0, waiting for transfers between devices: 44.4 us -> none  [the longest x1 25.2 us: local(): lax.all_to_all(sent_result, 'replica', split_axis=0, concat_axis=0, tiled...]
    dot_general x11 -> x0, matrix products: 18.4 us -> none  [the longest x2 7.06 us: partial(): jnp.einsum('shqk,skhd->sqhd', (weights / total).astype(jnp.bfloat16), spl...]
    unnamed x31 -> x9, local copies, waits for them, and re-layouts: 22 us -> 5.2 us
    all_to_all x3 -> x0, starting transfers between devices: 13.3 us -> none  [the longest x1 6.13 us: local(): lax.all_to_all(sent_result, 'replica', split_axis=0, concat_axis=0, tiled...]
    unnamed x1 -> x0, blocking collectives: 13.1 us -> none
    reduce_sum x6 -> x0, other arithmetic: 5.36 us -> none  [the longest x2 1.89 us: partial(): total = jnp.sum(weights, axis=-1, keepdims=True)]
    convert_element_type x3 -> x0, local copies, waits for them, and re-layouts: 5.03 us -> none  [the longest x1 3.44 us: local(): split_heads(pick_rows(receive_select, back_result)).astype(jnp.float32)]
  transfers between devices with their start and end apart: 3 -> 0, of which waited for: 2 -> 0; matrix products, arithmetic and copies ran while one was open for 20% -> 0% of each run, Pallas kernels for 0% -> 0%
where the time goes in v2:
time: 83.4 us; the launch traced here: 83.1 us
  Pallas kernels  75.8 us (91%)
  local copies, waits for them, and re-layouts  7.25 us (9%)
    pallas_call x1, Pallas kernels, local(): pl.pallas_call(functools.partial(kernel, peers, capacity, full_width), ou...  75.8 us
    unnamed x9, local copies, waits for them, and re-layouts  5.2 us

profile of v2, /device:TPU:0, one launch (start us, length us, event | category | flops | bytes accessed | tf_op | source)
XLA Modules:
  0.0 83.1 jit_solution(3023545846529412591)
XLA Ops:
  0.0 0.7 pad.4
  0.7 0.7 broadcast_in_dim.13.query_gain_ref
  1.4 0.7 broadcast_in_dim.14.key_gain_ref
  2.0 0.0 copy-start
  2.0 1.2 %copy-done = bf16[12,32,1280]{2,1,0:T(8,128)(2,1)S(1)} copy-done((bf16[12,32,1280]{2,1,0:T(8,128)(2,1)S(1)}, bf16[12,32,1280]{2,1,0:T(8,128)(2,1)}, u32[]{:S(2)}) %copy-start) | copy-done | bytes 983064
  3.2 0.0 copy-start.1
  3.3 1.2 %copy-done.1 = bf16[12,32,1280]{2,1,0:T(8,128)(2,1)S(1)} copy-done((bf16[12,32,1280]{2,1,0:T(8,128)(2,1)S(1)}, bf16[12,32,1280]{2,1,0:T(8,128)(2,1)}, u32[]{:S(2)}) %copy-start.1) | copy-done | bytes 983064
  4.5 0.0 copy-start.2
  4.5 1.2 %copy-done.2 = bf16[12,32,1280]{2,1,0:T(8,128)(2,1)S(1)} copy-done((bf16[12,32,1280]{2,1,0:T(8,128)(2,1)S(1)}, bf16[12,32,1280]{2,1,0:T(8,128)(2,1)}, u32[]{:S(2)}) %copy-start.2) | copy-done | bytes 983064
  5.7 0.0 copy-start.3
  5.7 0.7 copy-done.3
  6.3 75.8 %shard_map.91 = bf16[12,32,1280]{2,1,0:T(8,128)(2,1)S(1)} custom-call(s32[8,128]{1,0:T(8,128)S(1)} %broadcast_in_dim.12.row_ref, s32[12]{0:T(128)S(1)} %copy-done.3, bf16[12,32,1280]{2,1,0:T(8,128)(2,1)S(1)} %copy-done, bf16[12,32,1280]{2,1,0:T(8,128)(2,1)S(1)} %copy-done.1, bf16[12,32,1280]{2,1,0:T(8,128)(2,1)S(1)} %copy-done.2, ...), custom_call_target="tpu_custom_call" | custom-call | flops 314572800 | bytes 11796480 | tf_op jit(solution)/shard_map/pallas_call | solution.py:325
  82.1 0.9 %copy.11 = bf16[12,32,1280]{2,1,0:T(8,128)(2,1)} copy(bf16[12,32,1280]{2,1,0:T(8,128)(2,1)S(1)} %shard_map.91) | data formatting | bytes 1966080
  (1 shorter events, 0.0 us)
Async XLA Ops:
  2.0 1.2 %copy-start = (bf16[12,32,1280]{2,1,0:T(8,128)(2,1)S(1)}, bf16[12,32,1280]{2,1,0:T(8,128)(2,1)}, u32[]{:S(2)}) copy-start(bf16[12,32,1280]{2,1,0:T(8,128)(2,1)} %query_hbm.1) | copy-start | bytes 2949124
  3.2 1.2 %copy-start.1 = (bf16[12,32,1280]{2,1,0:T(8,128)(2,1)S(1)}, bf16[12,32,1280]{2,1,0:T(8,128)(2,1)}, u32[]{:S(2)}) copy-start(bf16[12,32,1280]{2,1,0:T(8,128)(2,1)} %key_hbm.1) | copy-start | bytes 2949124
  4.5 1.2 %copy-start.2 = (bf16[12,32,1280]{2,1,0:T(8,128)(2,1)S(1)}, bf16[12,32,1280]{2,1,0:T(8,128)(2,1)}, u32[]{:S(2)}) copy-start(bf16[12,32,1280]{2,1,0:T(8,128)(2,1)} %value_hbm.1) | copy-start | bytes 2949124
  5.7 0.7 copy-start.3

commit v3 on v2

v3 whole, which is shorter than its diff:
```python
import functools

import jax
import jax.numpy as jnp
from jax import lax
from jax.experimental import pallas as pl
from jax.experimental.pallas import tpu as pltpu
from jax.sharding import PartitionSpec as P

HEAD_DIM = 128
PAIR = 2 * HEAD_DIM
LANES = 128
MESH = pl.DeviceIdType.MESH
F32 = jnp.float32
BF16 = jnp.bfloat16


def pair_attention(queries, keys, values, valid):
    rows = queries.shape[0]
    zeros = jnp.zeros((rows, HEAD_DIM), queries.dtype)
    diagonal = jnp.concatenate(
        [
            jnp.concatenate([queries[:, :HEAD_DIM], zeros], axis=1),
            jnp.concatenate([zeros, queries[:, HEAD_DIM:]], axis=1),
        ],
        axis=0,
    )
    scores = lax.dot_general(
        diagonal, keys, (((1,), (1,)), ((), ())), preferred_element_type=F32
    ) * HEAD_DIM ** (-0.5)
    if valid is not None:
        scores = jnp.where(valid, scores, -1e30)
    top = jnp.max(scores, axis=1, keepdims=True)
    weights = jnp.exp(scores - top)
    total = jnp.sum(weights, axis=1, keepdims=True)
    result = jnp.dot(weights.astype(BF16), values, preferred_element_type=F32)
    inverse = 1.0 / total
    first = result[:rows, :HEAD_DIM] * inverse[:rows]
    second = result[rows:, HEAD_DIM:] * inverse[rows:]
    level = top + jnp.log(total)
    return jnp.concatenate([first, second], axis=1), level[:rows], level[rows:]


def kernel(
    peers,
    capacity,
    full_width,
    new_slot_ref,
    lengths_ref,
    query_hbm,
    key_hbm,
    value_hbm,
    cache_key_hbm,
    cache_value_hbm,
    query_gain_ref,
    key_gain_ref,
    out_ref,
    query,
    key,
    value,
    cache_key,
    cache_value,
    squares,
    squares_other,
    row,
    tables,
    sender_vmem,
    sender_picks,
    picks_vmem,
    picks,
    query_out,
    query_in,
    result_out,
    result_in,
    level_out,
    level_in,
    own_result,
    own_level,
    load_sem,
    square_sem,
    table_send,
    table_recv,
    query_send,
    query_recv,
    result_send,
    result_recv,
    level_send,
    level_recv,
):
    slots, block, width = query.shape
    pairs = width // PAIR
    me = lax.axis_index("replica")
    other = 1 - lax.axis_index("tensor")

    def peer(d):
        return lax.rem(me + d, peers)

    def order(k):
        half = (k + 1) // 2
        return jnp.where(lax.rem(k, 2) == 0, peers // 2 + half, peers // 2 - half)

    loads = [
        pltpu.make_async_copy(source, target, load_sem.at[n])
        for n, (source, target) in enumerate(
            (
                (query_hbm, query),
                (key_hbm, key),
                (value_hbm, value),
                (cache_key_hbm, cache_key),
                (cache_value_hbm, cache_value),
            )
        )
    ]
    loads[0].start()

    barrier = pltpu.get_barrier_semaphore()
    pl.semaphore_signal(barrier, inc=1, device_id={"tensor": other}, device_id_type=MESH)

    def greet(d, carry):
        pl.semaphore_signal(barrier, inc=1, device_id={"replica": peer(d)}, device_id_type=MESH)
        return carry

    lax.fori_loop(1, peers, greet, 0)
    tile_lane = lax.broadcasted_iota(jnp.int32, row.shape, 1)
    own_slots = jnp.full(row.shape, -1, jnp.int32)
    for j in range(slots):
        own_slots = jnp.where(tile_lane == j, new_slot_ref[j], own_slots)
    row[...] = own_slots
    tables[0] = own_slots
    pl.semaphore_wait(barrier, peers)

    def table_copy(d):
        return pltpu.make_async_remote_copy(
            src_ref=row,
            dst_ref=tables.at[d],
            send_sem=table_send.at[d],
            recv_sem=table_recv.at[d],
            device_id={"replica": peer(d)},
            device_id_type=MESH,
        )

    lax.fori_loop(1, peers, lambda d, carry: (table_copy(d).start(), carry)[1], 0)

    lane = lax.broadcasted_iota(jnp.int32, (block, LANES), 1)

    def sums_of(ref):
        sums = jnp.zeros((block, LANES), F32)
        for i in range(slots):
            rows = ref[i].astype(F32)
            sums = jnp.where(lane == i, jnp.sum(rows * rows, axis=1, keepdims=True), sums)
        return sums

    def exchange(n):
        return pltpu.make_async_remote_copy(
            src_ref=squares.at[n],
            dst_ref=squares_other.at[n],
            send_sem=square_sem.at[n, 0],
            recv_sem=square_sem.at[n, 1],
            device_id={"tensor": other},
            device_id_type=MESH,
        )

    def normalise(n, ref, gain_ref):
        exchange(n).wait()
        factors = lax.rsqrt((squares[n] + squares_other[n]) / full_width + 1e-06)
        gain = gain_ref[...].astype(F32).reshape(1, width)
        for i in range(slots):
            ref[i] = (ref[i].astype(F32) * factors[:, i : i + 1] * gain).astype(BF16)

    loads[0].wait()
    for load in loads[1:]:
        load.start()
    squares[0] = sums_of(query)
    exchange(0).start()

    lax.fori_loop(1, peers, lambda d, carry: (table_copy(d).wait_recv(), carry)[1], 0)
    board = tables[:, 0, :]
    shape = board.shape
    column = lax.broadcasted_iota(jnp.int32, shape, 1)
    sender = lax.broadcasted_iota(jnp.int32, shape, 0)
    mirrored = jnp.where(sender == 0, 0, peers - sender)
    mine = (board >= me * slots) & (board < me * slots + slots)
    chosen = jnp.zeros(shape, jnp.int32)
    places = jnp.zeros(shape, jnp.int32)
    for r in range(capacity):
        first = jnp.min(jnp.where(mine, column, LANES), axis=1, keepdims=True)
        now = mine & (column == first)
        local = jnp.max(jnp.where(now, board - me * slots, 0), axis=1, keepdims=True)
        chosen = jnp.where(column == r, local, chosen)
        places = jnp.where(now, mirrored * capacity + r, places)
        mine = mine & (column != first)
    sender_vmem[...] = chosen
    sender_scalars = pltpu.make_async_copy(sender_vmem, sender_picks, load_sem.at[5])
    sender_scalars.start()
    normalise(0, query, query_gain_ref)
    sender_scalars.wait()

    def query_copy(d):
        return pltpu.make_async_remote_copy(
            src_ref=query_out.at[d],
            dst_ref=query_in.at[d],
            send_sem=query_send.at[d],
            recv_sem=query_recv.at[d],
            device_id={"replica": peer(d)},
            device_id_type=MESH,
        )

    def result_copy(d):
        return pltpu.make_async_remote_copy(
            src_ref=result_out.at[d],
            dst_ref=result_in.at[d],
            send_sem=result_send.at[d],
            recv_sem=result_recv.at[d],
            device_id={"replica": lax.rem(me - d + peers, peers)},
            device_id_type=MESH,
        )

    def level_copy(d):
        return pltpu.make_async_remote_copy(
            src_ref=level_out.at[d],
            dst_ref=level_in.at[d],
            send_sem=level_send.at[d],
            recv_sem=level_recv.at[d],
            device_id={"replica": lax.rem(me - d + peers, peers)},
            device_id_type=MESH,
        )

    def send_queries(k, carry):
        d = order(k)
        for r in range(capacity):
            query_out[d, r] = query[sender_picks[peers - d, r]]
        query_copy(d).start()
        return carry

    lax.fori_loop(0, peers - 1, send_queries, 0)

    own_row = jnp.broadcast_to(tables[0][0:1], shape)
    back_base = lax.rem(me - sender + peers, peers) * slots
    theirs = (own_row >= back_base) & (own_row < back_base + slots)
    chosen = jnp.zeros(shape, jnp.int32)
    for r in range(capacity):
        first = jnp.min(jnp.where(theirs, column, LANES), axis=1, keepdims=True)
        chosen = jnp.where(column == r, jnp.where(first == LANES, 0, first), chosen)
        theirs = theirs & (column != first)
    for i in range(slots):
        matching = jnp.where(board == me * slots + i, places, 0)
        place = jnp.max(jnp.max(matching, axis=1, keepdims=True), axis=0, keepdims=True)
        chosen = jnp.where(column == capacity + i, place, chosen)
    picks_vmem[...] = chosen
    scalars = pltpu.make_async_copy(picks_vmem, picks, load_sem.at[6])
    scalars.start()
    loads[1].wait()
    squares[1] = sums_of(key)
    exchange(1).start()
    normalise(1, key, key_gain_ref)
    scalars.wait()
    for load in loads[2:]:
        load.wait()

    cached = cache_key.shape[1]
    position = lax.broadcasted_iota(jnp.int32, (2 * block, cached), 1)
    quarter = block // 4

    def visit(d, fetch, target, target_level):
        levels = jnp.zeros((block, LANES), F32)
        for r in range(capacity):
            g = picks[d, r]
            valid = position < lengths_ref[g]
            for c in range(pairs):
                part = slice(c * PAIR, (c + 1) * PAIR)
                result, even, odd = pair_attention(
                    fetch(r, part), cache_key[g, :, part], cache_value[g, :, part], valid
                )
                target[d, r, :, part] = result.astype(BF16)
                levels = jnp.where(lane == 16 * r + 2 * c, even, levels)
                levels = jnp.where(lane == 16 * r + 2 * c + 1, odd, levels)
        folded = levels[:quarter]
        for j in range(1, 4):
            folded = folded + pltpu.roll(levels[j * quarter : (j + 1) * quarter], 32 * j, 1)
        target_level[d] = folded

    def own_block(i, carry):
        levels = jnp.zeros((block, LANES), F32)
        for c in range(pairs):
            part = slice(c * PAIR, (c + 1) * PAIR)
            result, even, odd = pair_attention(
                query[i, :, part], key[i, :, part], value[i, :, part], None
            )
            own_result[i, :, part] = result
            levels = jnp.where(lane % 16 == 2 * c, even, levels)
            levels = jnp.where(lane % 16 == 2 * c + 1, odd, levels)
        own_level[i] = levels
        return carry

    def combine(d):
        folded = level_in[d]
        levels = jnp.concatenate(
            [folded] + [pltpu.roll(folded, LANES - 32 * j, 1) for j in range(1, 4)], axis=0
        )
        for r in range(capacity):
            i = sender_picks[lax.rem(peers - d, peers), r]
            share = 1.0 / (1.0 + jnp.exp(own_level[i] - levels))
            for h in range(width // HEAD_DIM):
                part = slice(h * HEAD_DIM, (h + 1) * HEAD_DIM)
                own = own_result[i, :, part]
                past = result_in[d, r, :, part].astype(F32)
                at = 16 * r + h
                mixed = own + share[:, at : at + 1] * (past - own)
                result_in[d, r, :, part] = mixed.astype(BF16)

    visit(0, lambda r, part: query[sender_picks[0, r], :, part], result_in, level_in)
    lax.fori_loop(0, slots, own_block, 0)

    def serve(k, carry):
        d = order(k)
        query_copy(d).wait_recv()
        visit(d, lambda r, part: query_in[d, r, :, part], result_out, level_out)
        level_copy(d).start()
        result_copy(d).start()
        return carry

    lax.fori_loop(0, peers - 1, serve, 0)
    combine(0)

    def collect(k, carry):
        d = order(k)
        level_copy(d).wait_recv()
        result_copy(d).wait_recv()
        combine(d)
        return carry

    lax.fori_loop(0, peers - 1, collect, 0)

    for i in range(slots):
        at = picks[0, capacity + i]
        out_ref[i] = result_in[at // capacity, lax.rem(at, capacity)]

    def finish_sends(d, carry):
        table_copy(d).wait_send()
        query_copy(d).wait_send()
        level_copy(d).wait_send()
        result_copy(d).wait_send()
        return carry

    lax.fori_loop(1, peers, finish_sends, 0)


def local(
    cache_keys,
    cache_values,
    lengths,
    new_slot,
    query_raw,
    block_keys_raw,
    block_values,
    query_gain,
    key_gain,
):
    slots, block, width = query_raw.shape
    cached = cache_keys.shape[1]
    peers = lax.axis_size("replica")
    capacity = -(-slots // peers)
    full_width = width * lax.axis_size("tensor")
    vmem = pl.BlockSpec(memory_space=pltpu.VMEM)
    smem = pl.BlockSpec(memory_space=pltpu.SMEM)
    hbm = pl.BlockSpec(memory_space=pl.ANY)
    message = (peers, capacity, block, width)
    level = (peers, block // 4, LANES)
    dma = pltpu.SemaphoreType.DMA
    return pl.pallas_call(
        functools.partial(kernel, peers, capacity, full_width),
        out_shape=jax.ShapeDtypeStruct(query_raw.shape, BF16),
        in_specs=[smem, smem, hbm, hbm, hbm, hbm, hbm, vmem, vmem],
        out_specs=vmem,
        scratch_shapes=[
            pltpu.VMEM(query_raw.shape, BF16),
            pltpu.VMEM(query_raw.shape, BF16),
            pltpu.VMEM(query_raw.shape, BF16),
            pltpu.VMEM(cache_keys.shape, BF16),
            pltpu.VMEM(cache_keys.shape, BF16),
            pltpu.VMEM((2, block, LANES), F32),
            pltpu.VMEM((2, block, LANES), F32),
            pltpu.VMEM((8, LANES), jnp.int32),
            pltpu.VMEM((peers, 8, LANES), jnp.int32),
            pltpu.VMEM((peers, LANES), jnp.int32),
            pltpu.SMEM((peers, LANES), jnp.int32),
            pltpu.VMEM((peers, LANES), jnp.int32),
            pltpu.SMEM((peers, LANES), jnp.int32),
            pltpu.VMEM(message, BF16),
            pltpu.VMEM(message, BF16),
            pltpu.VMEM(message, BF16),
            pltpu.VMEM(message, BF16),
            pltpu.VMEM(level, F32),
            pltpu.VMEM(level, F32),
            pltpu.VMEM(query_raw.shape, F32),
            pltpu.VMEM((slots, block, LANES), F32),
            dma((7,)),
            dma((2, 2)),
            dma((peers,)),
            dma((peers,)),
            dma((peers,)),
            dma((peers,)),
            dma((peers,)),
            dma((peers,)),
            dma((peers,)),
            dma((peers,)),
        ],
        compiler_params=pltpu.CompilerParams(
            collective_id=0, has_side_effects=True, vmem_limit_bytes=60 * 1024 * 1024
        ),
        cost_estimate=pl.CostEstimate(
            flops=4 * slots * block * (cached + block) * width,
            bytes_accessed=4 * cache_keys.size + 8 * query_raw.size,
            transcendentals=slots * block * (cached + block) * width // HEAD_DIM,
        ),
    )(
        new_slot,
        lengths,
        query_raw,
        block_keys_raw,
        block_values,
        cache_keys,
        cache_values,
        query_gain,
        key_gain,
    )


def solution(mesh):
    in_specs = (
        P(("groups", "replica"), None, "tensor"),
        P(("groups", "replica"), None, "tensor"),
        P(("groups", "replica")),
        P(("groups", "replica")),
        P(("groups", "replica"), None, "tensor"),
        P(("groups", "replica"), None, "tensor"),
        P(("groups", "replica"), None, "tensor"),
        P("tensor"),
        P("tensor"),
    )
    out_specs = P(("groups", "replica"), None, "tensor")
    return jax.shard_map(local, mesh=mesh, in_specs=in_specs, out_specs=out_specs, check_vma=False)
```

time: 83.4 us -> 74.1 us (0.89)
  local copies, waits for them, and re-layouts: 7.25 us -> 2.21 us
  Pallas kernels: 75.8 us -> 71.7 us
    pallas_call x1, Pallas kernels: 75.8 us -> 71.7 us  [local(): pl.pallas_call(functools.partial(kernel, peers, capacity, full_width), ou...]
    unnamed x9 -> x1, local copies, waits for them, and re-layouts: 5.2 us -> 2.21 us
    broadcast_in_dim x3 -> x0, local copies, waits for them, and re-layouts: 1.39 us -> none  [the longest x1 0.69 us: local(): query_gain[None]]
where the time goes in v3:
time: 74.1 us; the launch traced here: 73.9 us
  Pallas kernels  71.7 us (97%)
  local copies, waits for them, and re-layouts  2.21 us (3%)
    pallas_call x1, Pallas kernels, local(): pl.pallas_call(functools.partial(kernel, peers, capacity, full_width), ou...  71.7 us
    unnamed x1, local copies, waits for them, and re-layouts  2.21 us

profile of v3, /device:TPU:0, one launch (start us, length us, event | category | flops | bytes accessed | tf_op | source)
XLA Modules:
  0.0 73.9 jit_solution(9822925122014218962)
XLA Ops:
  0.0 71.7 %shard_map.91 = bf16[12,32,1280]{2,1,0:T(8,128)(2,1)} custom-call(s32[12]{0:T(128)} %new_slot_ref.1, s32[12]{0:T(128)} %lengths_ref.1, bf16[12,32,1280]{2,1,0:T(8,128)(2,1)} %query_hbm.1, bf16[12,32,1280]{2,1,0:T(8,128)(2,1)} %key_hbm.1, bf16[12,32,1280]{2,1,0:T(8,128)(2,1)} %value_hbm.1, bf16[12,128,1280]{2,1,0:T(8,128)(2,1)} %cache_key_hbm.1, ...), custom_call_target="tpu_custom_call" | custom-call | flops 314572800 | bytes 11796480 | tf_op jit(solution)/shard_map/pallas_call | solution.py:370
  71.7 2.2 %copy.11 = bf16[12,32,1280]{2,1,0:T(8,128)(2,1)} copy(bf16[12,32,1280]{2,1,0:T(8,128)(2,1)} %shard_map.91) | data formatting | bytes 1966080

commit v4 on v3

--- a/solution.py
+++ b/solution.py
@@ -93,11 +93,13 @@
     other = 1 - lax.axis_index("tensor")
 
     def peer(d):
-        return lax.rem(me + d, peers)
-
-    def order(k):
-        half = (k + 1) // 2
-        return jnp.where(lax.rem(k, 2) == 0, peers // 2 + half, peers // 2 - half)
+        partner, bit = 0, 1
+        while bit < peers:
+            partner = partner + lax.rem(me // bit + d // bit, 2) * bit
+            bit *= 2
+        return partner
+
+    half, quarter = peers // 2, peers // 4
 
     loads = [
         pltpu.make_async_copy(source, target, load_sem.at[n])
@@ -178,7 +180,6 @@
     shape = board.shape
     column = lax.broadcasted_iota(jnp.int32, shape, 1)
     sender = lax.broadcasted_iota(jnp.int32, shape, 0)
-    mirrored = jnp.where(sender == 0, 0, peers - sender)
     mine = (board >= me * slots) & (board < me * slots + slots)
     chosen = jnp.zeros(shape, jnp.int32)
     places = jnp.zeros(shape, jnp.int32)
@@ -187,7 +188,7 @@
         now = mine & (column == first)
         local = jnp.max(jnp.where(now, board - me * slots, 0), axis=1, keepdims=True)
         chosen = jnp.where(column == r, local, chosen)
-        places = jnp.where(now, mirrored * capacity + r, places)
+        places = jnp.where(now, sender * capacity + r, places)
         mine = mine & (column != first)
     sender_vmem[...] = chosen
     sender_scalars = pltpu.make_async_copy(sender_vmem, sender_picks, load_sem.at[5])
@@ -195,23 +196,23 @@
     normalise(0, query, query_gain_ref)
     sender_scalars.wait()
 
-    def query_copy(d):
+    def query_copy(d, r):
         return pltpu.make_async_remote_copy(
-            src_ref=query_out.at[d],
-            dst_ref=query_in.at[d],
-            send_sem=query_send.at[d],
-            recv_sem=query_recv.at[d],
+            src_ref=query_out.at[d, r],
+            dst_ref=query_in.at[d, r],
+            send_sem=query_send.at[d, r],
+            recv_sem=query_recv.at[d, r],
             device_id={"replica": peer(d)},
             device_id_type=MESH,
         )
 
-    def result_copy(d):
+    def result_copy(d, r):
         return pltpu.make_async_remote_copy(
-            src_ref=result_out.at[d],
-            dst_ref=result_in.at[d],
-            send_sem=result_send.at[d],
-            recv_sem=result_recv.at[d],
-            device_id={"replica": lax.rem(me - d + peers, peers)},
+            src_ref=result_out.at[d, r],
+            dst_ref=result_in.at[d, r],
+            send_sem=result_send.at[d, r],
+            recv_sem=result_recv.at[d, r],
+            device_id={"replica": peer(d)},
             device_id_type=MESH,
         )
 
@@ -221,21 +222,21 @@
             dst_ref=level_in.at[d],
             send_sem=level_send.at[d],
             recv_sem=level_recv.at[d],
-            device_id={"replica": lax.rem(me - d + peers, peers)},
+            device_id={"replica": peer(d)},
             device_id_type=MESH,
         )
 
-    def send_queries(k, carry):
-        d = order(k)
-        for r in range(capacity):
-            query_out[d, r] = query[sender_picks[peers - d, r]]
-        query_copy(d).start()
-        return carry
-
-    lax.fori_loop(0, peers - 1, send_queries, 0)
+    def send_queries(d, carry):
+        for r in range(capacity):
+            query_out[d, r] = query[sender_picks[d, r]]
+            query_copy(d, r).start()
+        return carry
+
+    lax.fori_loop(half, peers, send_queries, 0)
+    lax.fori_loop(1, half, send_queries, 0)
 
     own_row = jnp.broadcast_to(tables[0][0:1], shape)
-    back_base = lax.rem(me - sender + peers, peers) * slots
+    back_base = peer(sender) * slots
     theirs = (own_row >= back_base) & (own_row < back_base + slots)
     chosen = jnp.zeros(shape, jnp.int32)
     for r in range(capacity):
@@ -259,11 +260,13 @@
 
     cached = cache_key.shape[1]
     position = lax.broadcasted_iota(jnp.int32, (2 * block, cached), 1)
-    quarter = block // 4
-
-    def visit(d, fetch, target, target_level):
+    fold = block // 4
+
+    def visit(d, fetch, target, target_level, before=None, after=None):
         levels = jnp.zeros((block, LANES), F32)
         for r in range(capacity):
+            if before is not None:
+                before(d, r)
             g = picks[d, r]
             valid = position < lengths_ref[g]
             for c in range(pairs):
@@ -274,9 +277,11 @@
                 target[d, r, :, part] = result.astype(BF16)
                 levels = jnp.where(lane == 16 * r + 2 * c, even, levels)
                 levels = jnp.where(lane == 16 * r + 2 * c + 1, odd, levels)
-        folded = levels[:quarter]
+            if after is not None:
+                after(d, r)
+        folded = levels[:fold]
         for j in range(1, 4):
-            folded = folded + pltpu.roll(levels[j * quarter : (j + 1) * quarter], 32 * j, 1)
+            folded = folded + pltpu.roll(levels[j * fold : (j + 1) * fold], 32 * j, 1)
         target_level[d] = folded
 
     def own_block(i, carry):
@@ -298,7 +303,7 @@
             [folded] + [pltpu.roll(folded, LANES - 32 * j, 1) for j in range(1, 4)], axis=0
         )
         for r in range(capacity):
-            i = sender_picks[lax.rem(peers - d, peers), r]
+            i = sender_picks[d, r]
             share = 1.0 / (1.0 + jnp.exp(own_level[i] - levels))
             for h in range(width // HEAD_DIM):
                 part = slice(h * HEAD_DIM, (h + 1) * HEAD_DIM)
@@ -311,25 +316,29 @@
     visit(0, lambda r, part: query[sender_picks[0, r], :, part], result_in, level_in)
     lax.fori_loop(0, slots, own_block, 0)
 
-    def serve(k, carry):
-        d = order(k)
-        query_copy(d).wait_recv()
-        visit(d, lambda r, part: query_in[d, r, :, part], result_out, level_out)
+    def serve(d, carry):
+        visit(
+            d,
+            lambda r, part: query_in[d, r, :, part],
+            result_out,
+            level_out,
+            lambda d, r: query_copy(d, r).wait_recv(),
+            lambda d, r: result_copy(d, r).start(),
+        )
         level_copy(d).start()
-        result_copy(d).start()
-        return carry
-
-    lax.fori_loop(0, peers - 1, serve, 0)
+        return carry
+
+    lax.fori_loop(1, peers, serve, 0)
     combine(0)
 
-    def collect(k, carry):
-        d = order(k)
+    def collect(d, carry):
         level_copy(d).wait_recv()
-        result_copy(d).wait_recv()
+        for r in range(capacity):
+            result_copy(d, r).wait_recv()
         combine(d)
         return carry
 
-    lax.fori_loop(0, peers - 1, collect, 0)
+    lax.fori_loop(1, peers, collect, 0)
 
     for i in range(slots):
         at = picks[0, capacity + i]
@@ -337,12 +346,19 @@
 
     def finish_sends(d, carry):
         table_copy(d).wait_send()
-        query_copy(d).wait_send()
         level_copy(d).wait_send()
-        result_copy(d).wait_send()
+        for r in range(capacity):
+            result_copy(d, r).wait_send()
         return carry
 
     lax.fori_loop(1, peers, finish_sends, 0)
+
+    def finish_queries(d, carry):
+        for r in range(capacity):
+            query_copy(d, r).wait_send()
+        return carry
+
+    lax.fori_loop(1, peers, finish_queries, 0)
 
 
 def local(
@@ -398,10 +414,10 @@
             dma((2, 2)),
             dma((peers,)),
             dma((peers,)),
-            dma((peers,)),
-            dma((peers,)),
-            dma((peers,)),
-            dma((peers,)),
+            dma((peers, capacity)),
+            dma((peers, capacity)),
+            dma((peers, capacity)),
+            dma((peers, capacity)),
             dma((peers,)),
             dma((peers,)),
         ],

time: 74.1 us -> 72.5 us (0.978)
  the two profiles are of different devices: /device:TPU:0 before, /device:TPU:8 now
where the time goes in v4:
time: 72.5 us; the launch traced here: 72.3 us
  Pallas kernels  70.1 us (97%)
  local copies, waits for them, and re-layouts  2.21 us (3%)
    pallas_call x1, Pallas kernels, local(): pl.pallas_call(functools.partial(kernel, peers, capacity, full_width), ou...  70.1 us
    unnamed x1, local copies, waits for them, and re-layouts  2.21 us

profile of v4, /device:TPU:8, one launch (start us, length us, event | category | flops | bytes accessed | tf_op | source)
XLA Modules:
  0.0 72.3 jit_solution(2746966715310844103)
XLA Ops:
  0.0 70.1 %shard_map.91 = bf16[12,32,1280]{2,1,0:T(8,128)(2,1)} custom-call(s32[12]{0:T(128)} %new_slot_ref.1, s32[12]{0:T(128)} %lengths_ref.1, bf16[12,32,1280]{2,1,0:T(8,128)(2,1)} %query_hbm.1, bf16[12,32,1280]{2,1,0:T(8,128)(2,1)} %key_hbm.1, bf16[12,32,1280]{2,1,0:T(8,128)(2,1)} %value_hbm.1, bf16[12,128,1280]{2,1,0:T(8,128)(2,1)} %cache_key_hbm.1, ...), custom_call_target="tpu_custom_call" | custom-call | flops 314572800 | bytes 11796480 | tf_op jit(solution)/shard_map/pallas_call | solution.py:386
  70.1 2.2 %copy.11 = bf16[12,32,1280]{2,1,0:T(8,128)(2,1)} copy(bf16[12,32,1280]{2,1,0:T(8,128)(2,1)} %shard_map.91) | data formatting | bytes 1966080

commit v5 on v4

--- a/solution.py
+++ b/solution.py
@@ -76,6 +76,8 @@
     level_in,
     own_result,
     own_level,
+    placed,
+    out_sem,
     load_sem,
     square_sem,
     table_send,
@@ -174,6 +176,7 @@
         load.start()
     squares[0] = sums_of(query)
     exchange(0).start()
+    normalise(0, query, query_gain_ref)
 
     lax.fori_loop(1, peers, lambda d, carry: (table_copy(d).wait_recv(), carry)[1], 0)
     board = tables[:, 0, :]
@@ -193,7 +196,6 @@
     sender_vmem[...] = chosen
     sender_scalars = pltpu.make_async_copy(sender_vmem, sender_picks, load_sem.at[5])
     sender_scalars.start()
-    normalise(0, query, query_gain_ref)
     sender_scalars.wait()
 
     def query_copy(d, r):
@@ -342,7 +344,8 @@
 
     for i in range(slots):
         at = picks[0, capacity + i]
-        out_ref[i] = result_in[at // capacity, lax.rem(at, capacity)]
+        placed[i] = result_in[at // capacity, lax.rem(at, capacity)]
+        pltpu.make_async_copy(placed.at[i], out_ref.at[i], out_sem.at[i]).start()
 
     def finish_sends(d, carry):
         table_copy(d).wait_send()
@@ -352,6 +355,8 @@
         return carry
 
     lax.fori_loop(1, peers, finish_sends, 0)
+    for i in range(slots):
+        pltpu.make_async_copy(placed.at[i], out_ref.at[i], out_sem.at[i]).wait()
 
     def finish_queries(d, carry):
         for r in range(capacity):
@@ -387,7 +392,7 @@
         functools.partial(kernel, peers, capacity, full_width),
         out_shape=jax.ShapeDtypeStruct(query_raw.shape, BF16),
         in_specs=[smem, smem, hbm, hbm, hbm, hbm, hbm, vmem, vmem],
-        out_specs=vmem,
+        out_specs=hbm,
         scratch_shapes=[
             pltpu.VMEM(query_raw.shape, BF16),
             pltpu.VMEM(query_raw.shape, BF16),
@@ -410,6 +415,8 @@
             pltpu.VMEM(level, F32),
             pltpu.VMEM(query_raw.shape, F32),
             pltpu.VMEM((slots, block, LANES), F32),
+            pltpu.VMEM(query_raw.shape, BF16),
+            dma((slots,)),
             dma((7,)),
             dma((2, 2)),
             dma((peers,)),

time: 72.5 us -> 72.4 us (level)
  no operation moved by 1% of the time
where the time goes in v5:
time: 72.4 us; the launch traced here: 72.2 us
  Pallas kernels  70 us (97%)
  local copies, waits for them, and re-layouts  2.21 us (3%)
    pallas_call x1, Pallas kernels, local(): pl.pallas_call(functools.partial(kernel, peers, capacity, full_width), ou...  70 us
    unnamed x1, local copies, waits for them, and re-layouts  2.21 us

profile of v5, /device:TPU:8, one launch (start us, length us, event | category | flops | bytes accessed | tf_op | source)
XLA Modules:
  0.0 72.2 jit_solution(268362784301183798)
XLA Ops:
  0.0 70.0 %shard_map.91 = bf16[12,32,1280]{2,1,0:T(8,128)(2,1)} custom-call(s32[12]{0:T(128)} %new_slot_ref.1, s32[12]{0:T(128)} %lengths_ref.1, bf16[12,32,1280]{2,1,0:T(8,128)(2,1)} %query_hbm.1, bf16[12,32,1280]{2,1,0:T(8,128)(2,1)} %key_hbm.1, bf16[12,32,1280]{2,1,0:T(8,128)(2,1)} %value_hbm.1, bf16[12,128,1280]{2,1,0:T(8,128)(2,1)} %cache_key_hbm.1, ...), custom_call_target="tpu_custom_call" | custom-call | flops 314572800 | bytes 11796480 | tf_op jit(solution)/shard_map/pallas_call | solution.py:391
  70.0 2.2 %copy.11 = bf16[12,32,1280]{2,1,0:T(8,128)(2,1)} copy(bf16[12,32,1280]{2,1,0:T(8,128)(2,1)} %shard_map.91) | data formatting | bytes 1966080
